TPU v7x, 32 devices: a whole 2x2x4 slice. The times are simulated.
32 devices in a mesh: parts: 2 (over y), src: 4 (over x, core), space: 4 (over z).
Axes of the slice: x: 2, y: 2, z: 4, core: 2. Of those that a mesh axis runs over, the one named last changes fastest.
Arguments:
- fields: float32 [8, 4, 16, 128, 128], P(('parts', 'src'), None, 'space'), parts along dimension 0, may hold values from -6 to 6
- velocity: float32 [32, 128, 128], P(('parts', 'space')), parts along dimension 0, may hold values from 0.5 to 1
- conductivity: float32 [32, 128, 128], P(('parts', 'space')), parts along dimension 0, may hold values from 1 to 4
- labels: int32 [8], P(('parts', 'src')), parts along dimension 0, may hold values from 0 to 1, as said below
Outputs:
- fields_out: float32 [8, 2, 16, 128, 128], P(('parts', 'src'), None, 'space'), parts along dimension 0
- models_out: float32 [2, 32, 128, 128], P(None, ('parts', 'space')), parts along dimension 1
There are 2 independent parts, one for each index of `parts`. A program takes and returns all parts, laid end to end along the dimension named above; each array names one. Nothing has to cross between parts.
Inputs may be any that keep to these rules, and one draw needn't show every extreme that they name: `labels`: at least one group has label 0 and at least one has label 1; the rest are drawn.
All inputs are finite; a program needn't handle non-finite values.
Results may differ from a plain program's by a relative error of at most 0.00002.
Values sent between devices are 32-bit elements; how exact they have to be, the bound alone decides.
A program may use at most 64 MiB of HBM per device.

v0:
```python
import jax
import jax.numpy as jnp
from jax import lax
from jax.sharding import PartitionSpec as P

STEPS = 3


speed_gain = 0.25
diffuse_gain = 0.15
step_size = 0.1
penalty_gain = 50.0


def extended_2(block, sides, width):
    for axis, dim in sides:
        count = lax.axis_size(axis)
        forward = [(i, i + 1) for i in range(count - 1)]
        backward = [(target, source) for source, target in forward]
        low = lax.ppermute(
            lax.slice_in_dim(block, block.shape[dim] - width, None, axis=dim), axis, forward
        )
        high = lax.ppermute(lax.slice_in_dim(block, 0, width, axis=dim), axis, backward)
        block = jnp.concatenate([low, block, high], axis=dim)
    return block


def neighbours(padded):
    middle = padded[..., 1:-1, :, :]
    total = padded[..., 2:, :, :] + padded[..., :-2, :, :]
    zero_y = jnp.zeros_like(middle[..., :1, :])
    total = (
        total
        + jnp.concatenate([middle[..., 1:, :], zero_y], -2)
        + jnp.concatenate([zero_y, middle[..., :-1, :]], -2)
    )
    zero_z = jnp.zeros_like(middle[..., :1])
    total = (
        total
        + jnp.concatenate([middle[..., 1:], zero_z], -1)
        + jnp.concatenate([zero_z, middle[..., :-1]], -1)
    )
    return total - 6.0 * middle


def coefficient(weight, velocity, conductivity):
    return weight * speed_gain * velocity**2 + (1.0 - weight) * diffuse_gain / conductivity


def advance_thin(state, coef, weight):
    upper, upper_prev, lower, lower_prev = state
    accum = jnp.zeros_like(upper)
    for step in range(STEPS):
        padded = extended_2(jnp.stack([upper, lower], 1), (("space", 2),), 1)
        laps = neighbours(padded)
        lap_upper = laps[:, 0]
        lap_lower = laps[:, 1]
        accum = accum + lower * lap_upper
        upper_next = weight * (2.0 * upper - upper_prev) + (1.0 - weight) * upper + coef * lap_upper
        lower_next = weight * (2.0 * lower - lower_prev) + (1.0 - weight) * lower + coef * lap_lower
        upper_prev, upper = (upper, upper_next)
        lower_prev, lower = (lower, lower_next)
    return ((upper, upper_prev, lower, lower_prev), accum)


def advance(state, coef, weight):
    return advance_thin(state, coef, weight)


def penalty_term(velocity, conductivity):
    models = jnp.stack([velocity, jnp.log(conductivity)], 0)
    padded = extended_2(models, (("space", 1),), 1)
    middle = padded[:, 1:-1]
    first_idx = lax.axis_index("space")
    count = lax.axis_size("space")
    below = jnp.where(first_idx == 0, middle[:, :1], padded[:, :1])
    above = jnp.where(first_idx == count - 1, middle[:, -1:], padded[:, -1:])
    extended = jnp.concatenate([below, middle, above], 1)
    along_x = (extended[:, 2:] - extended[:, :-2]) * 0.5
    side = jnp.pad(middle, ((0, 0), (0, 0), (1, 1), (1, 1)), mode="edge")
    along_y = (side[:, :, 2:, 1:-1] - side[:, :, :-2, 1:-1]) * 0.5
    along_z = (side[:, :, 1:-1, 2:] - side[:, :, 1:-1, :-2]) * 0.5
    vx, lx = (along_x[0], along_x[1])
    vy, ly = (along_y[0], along_y[1])
    vz, lz = (along_z[0], along_z[1])
    cross_a = vy * lz - vz * ly
    cross_b = vz * lx - vx * lz
    cross_c = vx * ly - vy * lx
    return penalty_gain * (cross_a * cross_a + cross_b * cross_b + cross_c * cross_c)


def renew(velocity, conductivity, gradient, penalty):
    new_velocity = velocity * jnp.exp(-step_size * jnp.tanh(gradient[0] + penalty))
    new_conductivity = conductivity * jnp.exp(-step_size * jnp.tanh(gradient[1] + penalty))
    return jnp.stack([new_velocity, new_conductivity], 0)


def shards(fields, velocity, conductivity, labels):
    weight = labels.astype(jnp.float32).reshape(-1, 1, 1, 1)
    coef = coefficient(weight, velocity, conductivity)
    state = (fields[:, 0], fields[:, 1], fields[:, 2], fields[:, 3])
    state, accum = advance(state, coef, weight)
    penalty = penalty_term(velocity, conductivity)
    partial_sum = jnp.stack([jnp.sum(weight * accum, 0), jnp.sum((1.0 - weight) * accum, 0)], 0)
    groups_all = labels.shape[0] * lax.axis_size("src")
    scale = 1.0 / (20.0 * jnp.sqrt(jnp.float32(groups_all)))
    share = lax.psum_scatter(partial_sum, "src", scatter_dimension=2, tiled=True)
    band = share.shape[2]
    offset = lax.axis_index("src") * band
    vel_band = lax.dynamic_slice_in_dim(velocity, offset, band, 1)
    cond_band = lax.dynamic_slice_in_dim(conductivity, offset, band, 1)
    pen_band = lax.dynamic_slice_in_dim(penalty, offset, band, 1)
    fresh = renew(vel_band, cond_band, scale * share, pen_band)
    updated = lax.all_gather(fresh, "src", axis=2, tiled=True)
    coef_next = coefficient(weight, updated[0], updated[1])
    final, unused = advance(state, coef_next, weight)
    return (jnp.stack([final[0], final[2]], 1), updated)


def solution(mesh):
    in_specs = (
        P(("parts", "src"), None, "space", None, None),
        P(("parts", "space"), None, None),
        P(("parts", "space"), None, None),
        P(("parts", "src")),
    )
    out_specs = (
        P(("parts", "src"), None, "space", None, None),
        P(None, ("parts", "space"), None, None),
    )
    return jax.shard_map(shards, mesh=mesh, in_specs=in_specs, out_specs=out_specs, check_vma=False)
```

profile of v0, /device:TPU:0, one launch (start us, length us, event | category | flops | bytes accessed | tf_op | source)
XLA Modules:
  0.0 106.4 jit_solution(3605257124550417940)
XLA Ops:
  7.2 1.1 %fusion.140 = (f32[1,1,4,128,128]{4,3,2,1,0:T(8,128)S(1)}, f32[1,1,4,128,128]{4,3,2,1,0:T(8,128)S(1)}) fusion(f32[1,4,4,128,128]{4,3,2,1,0:T(8,128)} %param.4), kind=kLoop, calls=%fused_computation.300 | loop fusion | bytes 1048576 | tf_op jit(solution)/shard_map/slice | solution.py:101
  8.3 4.9 %collective-permute-start.1 = (f32[1,2,1,128,128]{4,3,2,1,0:T(8,128)S(1)}, f32[1,2,1,128,128]{4,3,2,1,0:T(8,128)S(1)}, u32[]{:S(2)}, u32[]{:S(2)}) collective-permute-start(f32[1,2,1,128,128]{4,3,2,1,0:T(8,128)S(1)} %get-tuple-element.69), channel_id=1, source_target_pairs={{0,1},{1,2},{2,3},{4,5},{5,6},{6,7},{8,9},{9,10},{10,11},{12,13},{... | collective-permute-start | bytes 393224 | tf_op jit(solution)/shard_map/ppermute | solution.py:20
  13.3 1.3 %collective-permute-start = (f32[1,2,1,128,128]{4,3,2,1,0:T(8,128)S(1)}, f32[1,2,1,128,128]{4,3,2,1,0:T(8,128)S(1)}, u32[]{:S(2)}, u32[]{:S(2)}) collective-permute-start(f32[1,2,1,128,128]{4,3,2,1,0:T(8,128)S(1)} %get-tuple-element.68), channel_id=1, source_target_pairs={{1,0},{2,1},{3,2},{5,4},{6,5},{7,6},{9,8},{10,9},{11,10},{13,12},{... | collective-permute-start | bytes 393224 | tf_op jit(solution)/shard_map/ppermute | solution.py:23
  15.5 0.5 collective-permute-done.1
  16.0 4.1 %collective-permute-done = f32[1,2,1,128,128]{4,3,2,1,0:T(8,128)S(1)} collective-permute-done((f32[1,2,1,128,128]{4,3,2,1,0:T(8,128)S(1)}, f32[1,2,1,128,128]{4,3,2,1,0:T(8,128)S(1)}, u32[]{:S(2)}, u32[]{:S(2)}) %collective-permute-start) | collective-permute-done | bytes 131104 | tf_op jit(solution)/shard_map/ppermute | solution.py:23
  20.1 0.3 fusion.35
  20.5 0.6 copy-done
  21.1 0.4 copy-done.1
  21.9 3.5 %collective-permute-start.3 = (f32[1,2,1,128,128]{4,3,2,1,0:T(8,128)S(1)}, f32[1,2,1,128,128]{4,3,2,1,0:T(8,128)S(1)}, u32[]{:S(2)}, u32[]{:S(2)}) collective-permute-start(f32[1,2,1,128,128]{4,3,2,1,0:T(8,128)S(1)} %get-tuple-element.63), channel_id=1, source_target_pairs={{0,1},{1,2},{2,3},{4,5},{5,6},{6,7},{8,9},{9,10},{10,11},{12,13},{... | collective-permute-start | bytes 393224 | tf_op jit(solution)/shard_map/ppermute | solution.py:20
  25.4 1.3 %collective-permute-start.2 = (f32[1,2,1,128,128]{4,3,2,1,0:T(8,128)S(1)}, f32[1,2,1,128,128]{4,3,2,1,0:T(8,128)S(1)}, u32[]{:S(2)}, u32[]{:S(2)}) collective-permute-start(f32[1,2,1,128,128]{4,3,2,1,0:T(8,128)S(1)} %get-tuple-element.62), channel_id=1, source_target_pairs={{1,0},{2,1},{3,2},{5,4},{6,5},{7,6},{9,8},{10,9},{11,10},{13,12},{... | collective-permute-start | bytes 393224 | tf_op jit(solution)/shard_map/ppermute | solution.py:23
  26.7 1.3 %collective-permute-start.6 = (f32[2,1,128,128]{3,2,1,0:T(8,128)S(1)}, f32[2,1,128,128]{3,2,1,0:T(8,128)S(1)}, u32[]{:S(2)}, u32[]{:S(2)}) collective-permute-start(f32[2,1,128,128]{3,2,1,0:T(8,128)S(1)} %pad_maximum_fusion.49), channel_id=1, source_target_pairs={{1,0},{2,1},{3,2},{5,4},{6,5},{7,6},{9,8},{10,9},{11,10},{13,12},{... | collective-permute-start | bytes 393224 | tf_op jit(solution)/shard_map/ppermute | solution.py:23
  28.1 0.2 fusion.141
  28.3 0.5 fusion.54
  28.9 0.8 fusion.142
  29.7 3.0 %collective-permute-done.2 = f32[1,2,1,128,128]{4,3,2,1,0:T(8,128)S(1)} collective-permute-done((f32[1,2,1,128,128]{4,3,2,1,0:T(8,128)S(1)}, f32[1,2,1,128,128]{4,3,2,1,0:T(8,128)S(1)}, u32[]{:S(2)}, u32[]{:S(2)}) %collective-permute-start.2) | collective-permute-done | bytes 131104 | tf_op jit(solution)/shard_map/ppermute | solution.py:23
  32.8 0.3 fusion.29
  33.3 3.6 %collective-permute-start.5 = (f32[1,2,1,128,128]{4,3,2,1,0:T(8,128)S(1)}, f32[1,2,1,128,128]{4,3,2,1,0:T(8,128)S(1)}, u32[]{:S(2)}, u32[]{:S(2)}) collective-permute-start(f32[1,2,1,128,128]{4,3,2,1,0:T(8,128)S(1)} %get-tuple-element.57), channel_id=1, source_target_pairs={{0,1},{1,2},{2,3},{4,5},{5,6},{6,7},{8,9},{9,10},{10,11},{12,13},{... | collective-permute-start | bytes 393224 | tf_op jit(solution)/shard_map/ppermute | solution.py:20
  36.9 1.3 %collective-permute-start.4 = (f32[1,2,1,128,128]{4,3,2,1,0:T(8,128)S(1)}, f32[1,2,1,128,128]{4,3,2,1,0:T(8,128)S(1)}, u32[]{:S(2)}, u32[]{:S(2)}) collective-permute-start(f32[1,2,1,128,128]{4,3,2,1,0:T(8,128)S(1)} %get-tuple-element.56), channel_id=1, source_target_pairs={{1,0},{2,1},{3,2},{5,4},{6,5},{7,6},{9,8},{10,9},{11,10},{13,12},{... | collective-permute-start | bytes 393224 | tf_op jit(solution)/shard_map/ppermute | solution.py:23
  38.5 4.6 %collective-permute-start.7 = (f32[2,1,128,128]{3,2,1,0:T(8,128)S(1)}, f32[2,1,128,128]{3,2,1,0:T(8,128)S(1)}, u32[]{:S(2)}, u32[]{:S(2)}) collective-permute-start(f32[2,1,128,128]{3,2,1,0:T(8,128)S(1)} %get-tuple-element.11), channel_id=1, source_target_pairs={{0,1},{1,2},{2,3},{4,5},{5,6},{6,7},{8,9},{9,10},{10,11},{12,13},{... | collective-permute-start | bytes 393224 | tf_op jit(solution)/shard_map/ppermute | solution.py:20
  43.1 0.7 collective-permute-done.4
  43.8 0.3 fusion.23
  44.1 0.2 multiply_bitcast_fusion.1
  44.4 0.8 pad_maximum_fusion.47
  45.3 2.4 %collective-permute-start.9 = (f32[1,2,1,128,128]{4,3,2,1,0:T(8,128)S(1)}, f32[1,2,1,128,128]{4,3,2,1,0:T(8,128)S(1)}, u32[]{:S(2)}, u32[]{:S(2)}) collective-permute-start(f32[1,2,1,128,128]{4,3,2,1,0:T(8,128)S(1)} %get-tuple-element.51), channel_id=1, source_target_pairs={{0,1},{1,2},{2,3},{4,5},{5,6},{6,7},{8,9},{9,10},{10,11},{12,13},{... | collective-permute-start | bytes 393224 | tf_op jit(solution)/shard_map/ppermute | solution.py:20
  47.7 1.3 %collective-permute-start.8 = (f32[1,2,1,128,128]{4,3,2,1,0:T(8,128)S(1)}, f32[1,2,1,128,128]{4,3,2,1,0:T(8,128)S(1)}, u32[]{:S(2)}, u32[]{:S(2)}) collective-permute-start(f32[1,2,1,128,128]{4,3,2,1,0:T(8,128)S(1)} %get-tuple-element.50), channel_id=1, source_target_pairs={{1,0},{2,1},{3,2},{5,4},{6,5},{7,6},{9,8},{10,9},{11,10},{13,12},{... | collective-permute-start | bytes 393224 | tf_op jit(solution)/shard_map/ppermute | solution.py:23
  49.4 0.8 collective-permute-done.9
  50.2 4.4 %collective-permute-done.8 = f32[1,2,1,128,128]{4,3,2,1,0:T(8,128)S(1)} collective-permute-done((f32[1,2,1,128,128]{4,3,2,1,0:T(8,128)S(1)}, f32[1,2,1,128,128]{4,3,2,1,0:T(8,128)S(1)}, u32[]{:S(2)}, u32[]{:S(2)}) %collective-permute-start.8) | collective-permute-done | bytes 131104 | tf_op jit(solution)/shard_map/ppermute | solution.py:23
  54.6 0.3 fusion.17
  54.9 11.3 %reduce-scatter.2.cloned.1.call-done = f32[2,4,32,128]{3,2,1,0:T(8,128)} async-done(((f32[2,4,128,128]{3,2,1,0:T(8,128)}), f32[2,4,32,128]{3,2,1,0:T(8,128)}) %reduce-scatter.2.cloned.1.call-update) | async-done | bytes 131088 | tf_op jit(solution)/shard_map/reduce_scatter | solution.py:107
  66.2 0.9 broadcast_multiply_fusion
  67.2 0.9 fusion.133
  68.1 6.8 %all_gather.3 = f32[2,4,128,128]{3,2,1,0:T(8,128)S(1)} all-gather(f32[2,4,32,128]{3,2,1,0:T(8,128)S(1)} %pad_maximum_fusion.51), channel_id=1, replica_groups=mesh['parts'=2,'src'=4,'space'=4] {'src'}, dimensions={2}, use_global_device_ids=true | all-gather | bytes 655360 | tf_op jit(solution)/shard_map/all_gather | solution.py:114
  75.1 0.2 fusion.8
  75.3 3.4 %collective-permute-start.11 = (f32[1,2,1,128,128]{4,3,2,1,0:T(8,128)S(1)}, f32[1,2,1,128,128]{4,3,2,1,0:T(8,128)S(1)}, u32[]{:S(2)}, u32[]{:S(2)}) collective-permute-start(f32[1,2,1,128,128]{4,3,2,1,0:T(8,128)S(1)} %get-tuple-element.37), channel_id=1, source_target_pairs={{0,1},{1,2},{2,3},{4,5},{5,6},{6,7},{8,9},{9,10},{10,11},{12,13},{... | collective-permute-start | bytes 393224 | tf_op jit(solution)/shard_map/ppermute | solution.py:20
  78.8 1.3 %collective-permute-start.10 = (f32[1,2,1,128,128]{4,3,2,1,0:T(8,128)S(1)}, f32[1,2,1,128,128]{4,3,2,1,0:T(8,128)S(1)}, u32[]{:S(2)}, u32[]{:S(2)}) collective-permute-start(f32[1,2,1,128,128]{4,3,2,1,0:T(8,128)S(1)} %get-tuple-element.36), channel_id=1, source_target_pairs={{1,0},{2,1},{3,2},{5,4},{6,5},{7,6},{9,8},{10,9},{11,10},{13,12},{... | collective-permute-start | bytes 393224 | tf_op jit(solution)/shard_map/ppermute | solution.py:23
  80.1 1.9 %collective-permute-done.11 = f32[1,2,1,128,128]{4,3,2,1,0:T(8,128)S(1)} collective-permute-done((f32[1,2,1,128,128]{4,3,2,1,0:T(8,128)S(1)}, f32[1,2,1,128,128]{4,3,2,1,0:T(8,128)S(1)}, u32[]{:S(2)}, u32[]{:S(2)}) %collective-permute-start.11) | collective-permute-done | bytes 131104 | tf_op jit(solution)/shard_map/ppermute | solution.py:20
  82.0 4.1 %collective-permute-done.10 = f32[1,2,1,128,128]{4,3,2,1,0:T(8,128)S(1)} collective-permute-done((f32[1,2,1,128,128]{4,3,2,1,0:T(8,128)S(1)}, f32[1,2,1,128,128]{4,3,2,1,0:T(8,128)S(1)}, u32[]{:S(2)}, u32[]{:S(2)}) %collective-permute-start.10) | collective-permute-done | bytes 131104 | tf_op jit(solution)/shard_map/ppermute | solution.py:23
  86.1 0.3 fusion.11
  86.4 0.3 fusion.134
  86.7 0.2 fusion.2
  86.9 3.4 %collective-permute-start.13 = (f32[1,2,1,128,128]{4,3,2,1,0:T(8,128)S(1)}, f32[1,2,1,128,128]{4,3,2,1,0:T(8,128)S(1)}, u32[]{:S(2)}, u32[]{:S(2)}) collective-permute-start(f32[1,2,1,128,128]{4,3,2,1,0:T(8,128)S(1)} %get-tuple-element.31), channel_id=1, source_target_pairs={{0,1},{1,2},{2,3},{4,5},{5,6},{6,7},{8,9},{9,10},{10,11},{12,13},{... | collective-permute-start | bytes 393224 | tf_op jit(solution)/shard_map/ppermute | solution.py:20
  90.3 1.3 %collective-permute-start.12 = (f32[1,2,1,128,128]{4,3,2,1,0:T(8,128)S(1)}, f32[1,2,1,128,128]{4,3,2,1,0:T(8,128)S(1)}, u32[]{:S(2)}, u32[]{:S(2)}) collective-permute-start(f32[1,2,1,128,128]{4,3,2,1,0:T(8,128)S(1)} %get-tuple-element.30), channel_id=1, source_target_pairs={{1,0},{2,1},{3,2},{5,4},{6,5},{7,6},{9,8},{10,9},{11,10},{13,12},{... | collective-permute-start | bytes 393224 | tf_op jit(solution)/shard_map/ppermute | solution.py:23
  91.7 1.1 %collective-permute-done.13 = f32[1,2,1,128,128]{4,3,2,1,0:T(8,128)S(1)} collective-permute-done((f32[1,2,1,128,128]{4,3,2,1,0:T(8,128)S(1)}, f32[1,2,1,128,128]{4,3,2,1,0:T(8,128)S(1)}, u32[]{:S(2)}, u32[]{:S(2)}) %collective-permute-start.13) | collective-permute-done | bytes 131104 | tf_op jit(solution)/shard_map/ppermute | solution.py:20
  92.8 4.4 %collective-permute-done.12 = f32[1,2,1,128,128]{4,3,2,1,0:T(8,128)S(1)} collective-permute-done((f32[1,2,1,128,128]{4,3,2,1,0:T(8,128)S(1)}, f32[1,2,1,128,128]{4,3,2,1,0:T(8,128)S(1)}, u32[]{:S(2)}, u32[]{:S(2)}) %collective-permute-start.12) | collective-permute-done | bytes 131104 | tf_op jit(solution)/shard_map/ppermute | solution.py:23
  97.2 0.3 fusion.5
  97.5 0.4 fusion.77
  97.9 0.8 pad_maximum_fusion.48
  98.8 0.8 copy.8
  (41 shorter events, 2.3 us)
Async XLA Ops:
  7.2 59.1 %reduce-scatter.2.cloned.1.call-start = ((), (), s32[]{:S(2)}) async-start(), calls=%async_computation.1 | async-start | bytes 655360 | tf_op jit(solution)/shard_map/reduce_scatter | solution.py:107
  8.3 7.7 %collective-permute-start.1 = (f32[1,2,1,128,128]{4,3,2,1,0:T(8,128)S(1)}, f32[1,2,1,128,128]{4,3,2,1,0:T(8,128)S(1)}, u32[]{:S(2)}, u32[]{:S(2)}) collective-permute-start(f32[1,2,1,128,128]{4,3,2,1,0:T(8,128)S(1)} %get-tuple-element.69), channel_id=1, source_target_pairs={{0,1},{1,2},{2,3},{4,5},{5,6},{6,7},{8,9},{9,10},{10,11},{12,13},{... | collective-permute-start | bytes 393224 | tf_op jit(solution)/shard_map/ppermute | solution.py:20
  13.3 6.9 %collective-permute-start = (f32[1,2,1,128,128]{4,3,2,1,0:T(8,128)S(1)}, f32[1,2,1,128,128]{4,3,2,1,0:T(8,128)S(1)}, u32[]{:S(2)}, u32[]{:S(2)}) collective-permute-start(f32[1,2,1,128,128]{4,3,2,1,0:T(8,128)S(1)} %get-tuple-element.68), channel_id=1, source_target_pairs={{1,0},{2,1},{3,2},{5,4},{6,5},{7,6},{9,8},{10,9},{11,10},{13,12},{... | collective-permute-start | bytes 393224 | tf_op jit(solution)/shard_map/ppermute | solution.py:23
  20.1 1.0 copy-start
  20.1 1.3 %copy-start.1 = (f32[1,4,4,128,128]{4,3,2,1,0:T(8,128)S(1)}, f32[1,4,4,128,128]{4,3,2,1,0:T(8,128)}, u32[]{:S(2)}) copy-start(f32[1,4,4,128,128]{4,3,2,1,0:T(8,128)} %param.4) | copy-start | bytes 3145732
  20.1 1.3 %copy-start.2 = (f32[4,128,128]{2,1,0:T(8,128)S(1)}, f32[4,128,128]{2,1,0:T(8,128)}, u32[]{:S(2)}) copy-start(f32[4,128,128]{2,1,0:T(8,128)} %param.6) | copy-start | bytes 786436
  21.9 7.8 %collective-permute-start.3 = (f32[1,2,1,128,128]{4,3,2,1,0:T(8,128)S(1)}, f32[1,2,1,128,128]{4,3,2,1,0:T(8,128)S(1)}, u32[]{:S(2)}, u32[]{:S(2)}) collective-permute-start(f32[1,2,1,128,128]{4,3,2,1,0:T(8,128)S(1)} %get-tuple-element.63), channel_id=1, source_target_pairs={{0,1},{1,2},{2,3},{4,5},{5,6},{6,7},{8,9},{9,10},{10,11},{12,13},{... | collective-permute-start | bytes 393224 | tf_op jit(solution)/shard_map/ppermute | solution.py:20
  25.4 7.3 %collective-permute-start.2 = (f32[1,2,1,128,128]{4,3,2,1,0:T(8,128)S(1)}, f32[1,2,1,128,128]{4,3,2,1,0:T(8,128)S(1)}, u32[]{:S(2)}, u32[]{:S(2)}) collective-permute-start(f32[1,2,1,128,128]{4,3,2,1,0:T(8,128)S(1)} %get-tuple-element.62), channel_id=1, source_target_pairs={{1,0},{2,1},{3,2},{5,4},{6,5},{7,6},{9,8},{10,9},{11,10},{13,12},{... | collective-permute-start | bytes 393224 | tf_op jit(solution)/shard_map/ppermute | solution.py:23
  26.7 11.7 %collective-permute-start.6 = (f32[2,1,128,128]{3,2,1,0:T(8,128)S(1)}, f32[2,1,128,128]{3,2,1,0:T(8,128)S(1)}, u32[]{:S(2)}, u32[]{:S(2)}) collective-permute-start(f32[2,1,128,128]{3,2,1,0:T(8,128)S(1)} %pad_maximum_fusion.49), channel_id=1, source_target_pairs={{1,0},{2,1},{3,2},{5,4},{6,5},{7,6},{9,8},{10,9},{11,10},{13,12},{... | collective-permute-start | bytes 393224 | tf_op jit(solution)/shard_map/ppermute | solution.py:23
  33.3 9.8 %collective-permute-start.5 = (f32[1,2,1,128,128]{4,3,2,1,0:T(8,128)S(1)}, f32[1,2,1,128,128]{4,3,2,1,0:T(8,128)S(1)}, u32[]{:S(2)}, u32[]{:S(2)}) collective-permute-start(f32[1,2,1,128,128]{4,3,2,1,0:T(8,128)S(1)} %get-tuple-element.57), channel_id=1, source_target_pairs={{0,1},{1,2},{2,3},{4,5},{5,6},{6,7},{8,9},{9,10},{10,11},{12,13},{... | collective-permute-start | bytes 393224 | tf_op jit(solution)/shard_map/ppermute | solution.py:20
  36.9 6.9 %collective-permute-start.4 = (f32[1,2,1,128,128]{4,3,2,1,0:T(8,128)S(1)}, f32[1,2,1,128,128]{4,3,2,1,0:T(8,128)S(1)}, u32[]{:S(2)}, u32[]{:S(2)}) collective-permute-start(f32[1,2,1,128,128]{4,3,2,1,0:T(8,128)S(1)} %get-tuple-element.56), channel_id=1, source_target_pairs={{1,0},{2,1},{3,2},{5,4},{6,5},{7,6},{9,8},{10,9},{11,10},{13,12},{... | collective-permute-start | bytes 393224 | tf_op jit(solution)/shard_map/ppermute | solution.py:23
  38.5 10.5 %collective-permute-start.7 = (f32[2,1,128,128]{3,2,1,0:T(8,128)S(1)}, f32[2,1,128,128]{3,2,1,0:T(8,128)S(1)}, u32[]{:S(2)}, u32[]{:S(2)}) collective-permute-start(f32[2,1,128,128]{3,2,1,0:T(8,128)S(1)} %get-tuple-element.11), channel_id=1, source_target_pairs={{0,1},{1,2},{2,3},{4,5},{5,6},{6,7},{8,9},{9,10},{10,11},{12,13},{... | collective-permute-start | bytes 393224 | tf_op jit(solution)/shard_map/ppermute | solution.py:20
  45.3 4.9 %collective-permute-start.9 = (f32[1,2,1,128,128]{4,3,2,1,0:T(8,128)S(1)}, f32[1,2,1,128,128]{4,3,2,1,0:T(8,128)S(1)}, u32[]{:S(2)}, u32[]{:S(2)}) collective-permute-start(f32[1,2,1,128,128]{4,3,2,1,0:T(8,128)S(1)} %get-tuple-element.51), channel_id=1, source_target_pairs={{0,1},{1,2},{2,3},{4,5},{5,6},{6,7},{8,9},{9,10},{10,11},{12,13},{... | collective-permute-start | bytes 393224 | tf_op jit(solution)/shard_map/ppermute | solution.py:20
  47.7 6.9 %collective-permute-start.8 = (f32[1,2,1,128,128]{4,3,2,1,0:T(8,128)S(1)}, f32[1,2,1,128,128]{4,3,2,1,0:T(8,128)S(1)}, u32[]{:S(2)}, u32[]{:S(2)}) collective-permute-start(f32[1,2,1,128,128]{4,3,2,1,0:T(8,128)S(1)} %get-tuple-element.50), channel_id=1, source_target_pairs={{1,0},{2,1},{3,2},{5,4},{6,5},{7,6},{9,8},{10,9},{11,10},{13,12},{... | collective-permute-start | bytes 393224 | tf_op jit(solution)/shard_map/ppermute | solution.py:23
  75.3 6.7 %collective-permute-start.11 = (f32[1,2,1,128,128]{4,3,2,1,0:T(8,128)S(1)}, f32[1,2,1,128,128]{4,3,2,1,0:T(8,128)S(1)}, u32[]{:S(2)}, u32[]{:S(2)}) collective-permute-start(f32[1,2,1,128,128]{4,3,2,1,0:T(8,128)S(1)} %get-tuple-element.37), channel_id=1, source_target_pairs={{0,1},{1,2},{2,3},{4,5},{5,6},{6,7},{8,9},{9,10},{10,11},{12,13},{... | collective-permute-start | bytes 393224 | tf_op jit(solution)/shard_map/ppermute | solution.py:20
  78.8 7.4 %collective-permute-start.10 = (f32[1,2,1,128,128]{4,3,2,1,0:T(8,128)S(1)}, f32[1,2,1,128,128]{4,3,2,1,0:T(8,128)S(1)}, u32[]{:S(2)}, u32[]{:S(2)}) collective-permute-start(f32[1,2,1,128,128]{4,3,2,1,0:T(8,128)S(1)} %get-tuple-element.36), channel_id=1, source_target_pairs={{1,0},{2,1},{3,2},{5,4},{6,5},{7,6},{9,8},{10,9},{11,10},{13,12},{... | collective-permute-start | bytes 393224 | tf_op jit(solution)/shard_map/ppermute | solution.py:23
  86.9 5.9 %collective-permute-start.13 = (f32[1,2,1,128,128]{4,3,2,1,0:T(8,128)S(1)}, f32[1,2,1,128,128]{4,3,2,1,0:T(8,128)S(1)}, u32[]{:S(2)}, u32[]{:S(2)}) collective-permute-start(f32[1,2,1,128,128]{4,3,2,1,0:T(8,128)S(1)} %get-tuple-element.31), channel_id=1, source_target_pairs={{0,1},{1,2},{2,3},{4,5},{5,6},{6,7},{8,9},{9,10},{10,11},{12,13},{... | collective-permute-start | bytes 393224 | tf_op jit(solution)/shard_map/ppermute | solution.py:20
  90.3 6.9 %collective-permute-start.12 = (f32[1,2,1,128,128]{4,3,2,1,0:T(8,128)S(1)}, f32[1,2,1,128,128]{4,3,2,1,0:T(8,128)S(1)}, u32[]{:S(2)}, u32[]{:S(2)}) collective-permute-start(f32[1,2,1,128,128]{4,3,2,1,0:T(8,128)S(1)} %get-tuple-element.30), channel_id=1, source_target_pairs={{1,0},{2,1},{3,2},{5,4},{6,5},{7,6},{9,8},{10,9},{11,10},{13,12},{... | collective-permute-start | bytes 393224 | tf_op jit(solution)/shard_map/ppermute | solution.py:23
Sparse Core Ops, SparseCore 0:
  45.4 20.8 reduce-scatter.1
where the time goes:
time: 107 us; the launch traced here: 106 us
  waiting for transfers between devices  36.2 us (34%)
  starting transfers between devices  34.9 us (33%)
  between operations  15.1 us (14%)
  other arithmetic  9.47 us (9%)
  blocking collectives  6.77 us (6%)
  local copies, waits for them, and re-layouts  3.91 us (4%)
    ppermute x7, starting transfers between devices, extended_2(): lax.ppermute(lax.slice_in_dim(block, block.shape[dim] - width, None, axis...  25.9 us
    ppermute x7, waiting for transfers between devices, extended_2(): lax.ppermute(lax.slice_in_dim(block, 0, width, axis=dim), axis, backward)  20.7 us
    reduce_scatter x1, waiting for transfers between devices, shards(): lax.psum_scatter(partial_sum, 'src', scatter_dimension=2, tiled=True)  11.3 us
    ppermute x7, starting transfers between devices, extended_2(): lax.ppermute(lax.slice_in_dim(block, 0, width, axis=dim), axis, backward)  9.04 us
    all_gather x1, blocking collectives, shards(): updated = lax.all_gather(fresh, 'src', axis=2, tiled=True)  6.77 us
    ppermute x7, waiting for transfers between devices, extended_2(): lax.ppermute(lax.slice_in_dim(block, block.shape[dim] - width, None, axis...  4.21 us
    another operation x21, other arithmetic, advance_thin(): padded = extended_2(jnp.stack([upper, lower], 1), (('space', 2),), 1)  2.26 us
  transfers between devices with their start and end apart: 15, of which 11 were waited for; matrix products, arithmetic and copies ran while one was open for 5% of the time, Pallas kernels for 0%

commit v1 on v0

v1 whole, which is shorter than its diff:
```python
import functools
import math

import jax
import jax.numpy as jnp
from jax import lax
from jax.experimental import pallas as pl
from jax.experimental.pallas import tpu as pltpu
from jax.sharding import PartitionSpec as P

STEPS = 3
PAD = 8
MESH = pl.DeviceIdType.MESH

speed_gain = 0.25
diffuse_gain = 0.15
step_size = 0.1
penalty_gain = 50.0


def coefficient(weight, velocity, conductivity):
    return weight * speed_gain * velocity**2 + (1.0 - weight) * diffuse_gain / conductivity


def kernel(
    spaces, srcs, groups,
    fields, velocity, conductivity, labels,
    fields_out, models_out,
    state, prev, halo, models, near, window, pen, coef, acc, got, label_own, label_got, fresh, updated, final,
    load_sem, model_sem, out_sem,
    halo_send, halo_recv, near_send, near_recv,
    label_send, label_recv, grad_send, grad_recv, fresh_send, fresh_recv,
):
    planes, ny, nz = fields.shape[2:]
    band = ny // srcs
    rows = 32 if ny % 32 == 0 else 8
    last = 2 * STEPS
    tile = lax.axis_index("space")
    me = lax.axis_index("src")
    offset = pl.multiple_of(me * band, 8)
    has_low = tile > 0
    has_high = tile < spaces - 1
    sides = ((has_low, tile - 1), (has_high, tile + 1))
    peers = [lax.rem(me + d, srcs) for d in range(1, srcs)]
    inner = list(range(1, planes - 1))
    edge = [0, planes - 1]
    slot = {p: p - 1 for p in inner}
    slot[0] = planes - 2
    slot[planes - 1] = planes - 1
    parts = ((0, planes - 2), (planes - 2, 2))

    loads = []
    for f in range(2):
        loads.append(pltpu.make_async_copy(
            fields.at[0, 2 * f], state.at[0, f, :, pl.ds(PAD, ny), :], load_sem.at[2 * f]))
        loads.append(pltpu.make_async_copy(fields.at[0, 2 * f + 1], prev.at[f], load_sem.at[2 * f + 1]))
    model_loads = [
        pltpu.make_async_copy(ref, models.at[m, :, pl.ds(PAD, ny), :], model_sem.at[m])
        for m, ref in enumerate((velocity, conductivity))
    ]
    for copy in loads + model_loads:
        copy.start()

    barrier = pltpu.get_barrier_semaphore()
    for exists, other in sides:
        @pl.when(exists)
        def _():
            pl.semaphore_signal(barrier, inc=1, device_id={"space": other}, device_id_type=MESH)
    for peer in peers:
        pl.semaphore_signal(barrier, inc=1, device_id={"src": peer}, device_id_type=MESH)

    weight = labels[0].astype(jnp.float32)
    label_own[...] = jnp.full(label_own.shape, weight, jnp.float32)
    lane = lax.broadcasted_iota(jnp.int32, (1, nz), 1)
    first_lane = lane == 0
    last_lane = lane == nz - 1
    zero_rows = jnp.zeros((PAD, nz), jnp.float32)
    for k in range(last):
        for f in range(2):
            for p in range(planes):
                state[k, f, p, pl.ds(0, PAD), :] = zero_rows
                state[k, f, p, pl.ds(PAD + ny, PAD), :] = zero_rows

    pl.semaphore_wait(barrier, srcs - 1 + has_low.astype(jnp.int32) + has_high.astype(jnp.int32))

    def halo_copy(k, f, side):
        plane = 0 if side == 0 else planes - 1
        if k == 0:
            source = fields.at[0, 2 * f, plane]
        else:
            source = state.at[k, f, plane, pl.ds(PAD, ny), :]
        return pltpu.make_async_remote_copy(
            src_ref=source, dst_ref=halo.at[k, f, 1 - side],
            send_sem=halo_send.at[k, f, side], recv_sem=halo_recv.at[k, f, 1 - side],
            device_id={"space": sides[side][1]}, device_id_type=MESH)

    def halo_start(k, f):
        for side in range(2):
            @pl.when(sides[side][0])
            def _():
                halo_copy(k, f, side).start()

    def halo_wait(k, f, side):
        @pl.when(sides[side][0])
        def _():
            pltpu.make_async_remote_copy(
                src_ref=halo.at[k, f, side], dst_ref=halo.at[k, f, side],
                send_sem=halo_send.at[k, f, side], recv_sem=halo_recv.at[k, f, side],
                device_id={"space": sides[side][1]}, device_id_type=MESH).wait_recv()

    def near_copy(m, side):
        ref = (velocity, conductivity)[m]
        plane = 0 if side == 0 else planes - 1
        return pltpu.make_async_remote_copy(
            src_ref=ref.at[plane, pl.ds(offset, band), :], dst_ref=near.at[m, 1 - side],
            send_sem=near_send.at[m, side], recv_sem=near_recv.at[m, 1 - side],
            device_id={"space": sides[side][1]}, device_id_type=MESH)

    def near_wait(m, side):
        pltpu.make_async_remote_copy(
            src_ref=near.at[m, side], dst_ref=near.at[m, side],
            send_sem=near_send.at[m, side], recv_sem=near_recv.at[m, side],
            device_id={"space": sides[side][1]}, device_id_type=MESH).wait_recv()

    def label_copy(d):
        return pltpu.make_async_remote_copy(
            src_ref=label_own, dst_ref=label_got.at[d],
            send_sem=label_send.at[d], recv_sem=label_recv.at[d],
            device_id={"src": peers[d]}, device_id_type=MESH)

    def grad_copy(part, d):
        begin, count = parts[part]
        return pltpu.make_async_remote_copy(
            src_ref=acc.at[pl.ds(begin, count), pl.ds(pl.multiple_of(peers[d] * band, 8), band), :],
            dst_ref=got.at[d, pl.ds(begin, count)],
            send_sem=grad_send.at[part, d], recv_sem=grad_recv.at[part, d],
            device_id={"src": peers[d]}, device_id_type=MESH)

    def fresh_copy(part, d):
        begin, count = parts[part]
        return pltpu.make_async_remote_copy(
            src_ref=fresh.at[:, pl.ds(begin, count)],
            dst_ref=updated.at[:, pl.ds(begin, count), pl.ds(offset, band), :],
            send_sem=fresh_send.at[part, d], recv_sem=fresh_recv.at[part, d],
            device_id={"src": peers[d]}, device_id_type=MESH)

    def fresh_wait(part, d):
        begin, count = parts[part]
        source = pl.multiple_of(lax.rem(me + srcs - 1 - d, srcs) * band, 8)
        ref = updated.at[:, pl.ds(begin, count), pl.ds(source, band), :]
        pltpu.make_async_remote_copy(
            src_ref=ref, dst_ref=ref,
            send_sem=fresh_send.at[part, d], recv_sem=fresh_recv.at[part, d],
            device_id={"src": peers[d]}, device_id_type=MESH).wait_recv()

    halo_start(0, 0)
    halo_start(0, 1)
    for side in range(2):
        @pl.when(sides[side][0])
        def _():
            for m in range(2):
                near_copy(m, side).start()
    for d in range(srcs - 1):
        label_copy(d).start()

    for side in range(2):
        @pl.when(jnp.logical_not(sides[side][0]))
        def _():
            for k in range(last):
                for f in range(2):
                    halo[k, f, side] = jnp.zeros((ny, nz), jnp.float32)

    def in_rows(body):
        def step(i, carry):
            body(pl.multiple_of(i * rows, 8))
            return carry
        lax.fori_loop(0, ny // rows, step, 0, unroll=True)

    keep_gain = 1.0 + weight

    def advance(k, f, p):
        def body(r):
            def at(plane, shift):
                return state[k, f, plane, pl.ds(r + PAD + shift, rows), :]
            middle = at(p, 0)
            below = halo[k, f, 0, pl.ds(r, rows), :] if p == 0 else at(p - 1, 0)
            above = halo[k, f, 1, pl.ds(r, rows), :] if p == planes - 1 else at(p + 1, 0)
            total = below + above
            total = total + at(p, 1) + at(p, -1)
            right = jnp.where(last_lane, 0.0, pltpu.roll(middle, nz - 1, 1))
            left = jnp.where(first_lane, 0.0, pltpu.roll(middle, 1, 1))
            lap = total + right + left - 6.0 * middle
            if f == 0 and k < STEPS:
                term = state[k, 1, p, pl.ds(r + PAD, rows), :] * lap
                if k == 0:
                    acc[slot[p], pl.ds(r, rows), :] = term
                else:
                    acc[slot[p], pl.ds(r, rows), :] += term
            if k == 0:
                before = prev[f, p, pl.ds(r, rows), :]
            else:
                before = state[k - 1, f, p, pl.ds(r + PAD, rows), :]
            value = keep_gain * middle - weight * before + coef[slot[p], pl.ds(r, rows), :] * lap
            if k == last - 1:
                final[f, p, pl.ds(r, rows), :] = value
            else:
                state[k + 1, f, p, pl.ds(r + PAD, rows), :] = value
        in_rows(body)

    def out_copy(f, p):
        return pltpu.make_async_copy(final.at[f, p], fields_out.at[0, f, p], out_sem.at[f, p])

    def model_out_copy(m, p):
        return pltpu.make_async_copy(updated.at[m, slot[p]], models_out.at[m, p], out_sem.at[2 + m, p])

    def form_coef(p, velocity_at, conductivity_at):
        def body(r):
            coef[slot[p], pl.ds(r, rows), :] = coefficient(weight, velocity_at(p, r), conductivity_at(p, r))
        in_rows(body)

    for copy in model_loads:
        copy.wait()
    for p in range(planes):
        form_coef(
            p,
            lambda p, r: models[0, p, pl.ds(r + PAD, rows), :],
            lambda p, r: models[1, p, pl.ds(r + PAD, rows), :],
        )
        for m in range(2):
            models[m, p, pl.ds(0, PAD), :] = jnp.broadcast_to(models[m, p, pl.ds(PAD, 1), :], (PAD, nz))
            models[m, p, pl.ds(PAD + ny, PAD), :] = jnp.broadcast_to(
                models[m, p, pl.ds(PAD + ny - 1, 1), :], (PAD, nz))
    for copy in loads:
        copy.wait()

    def boundary(k, f):
        for side in range(2):
            halo_wait(k, f, side)
            advance(k, f, edge[side])
            if k + 1 < last:
                @pl.when(sides[side][0])
                def _():
                    halo_copy(k + 1, f, side).start()
            else:
                out_copy(f, edge[side]).start()

    def interior(k, f):
        for p in inner:
            advance(k, f, p)
            if k == last - 1:
                out_copy(f, p).start()

    def penalty():
        def prepare(p, carry):
            window[0, p] = models[0, p, pl.ds(offset, band + 2 * PAD), :]
            window[1, p] = jnp.log(models[1, p, pl.ds(offset, band + 2 * PAD), :])
            return carry
        for p in range(planes):
            prepare(p, 0)
        for side in range(2):
            @pl.when(sides[side][0])
            def _():
                for m in range(2):
                    near_wait(m, side)
                near[1, side] = jnp.log(near[1, side])

            @pl.when(jnp.logical_not(sides[side][0]))
            def _():
                for m in range(2):
                    near[m, side] = window[m, edge[side], pl.ds(PAD, band), :]
        for p in range(planes):
            diffs = []
            for m in range(2):
                middle = window[m, p, pl.ds(PAD, band), :]
                below = near[m, 0] if p == 0 else window[m, p - 1, pl.ds(PAD, band), :]
                above = near[m, 1] if p == planes - 1 else window[m, p + 1, pl.ds(PAD, band), :]
                dx = (above - below) * 0.5
                dy = (window[m, p, pl.ds(PAD + 1, band), :] - window[m, p, pl.ds(PAD - 1, band), :]) * 0.5
                right = jnp.where(last_lane, middle, pltpu.roll(middle, nz - 1, 1))
                left = jnp.where(first_lane, middle, pltpu.roll(middle, 1, 1))
                diffs.append((dx, dy, (right - left) * 0.5))
            (vx, vy, vz), (lx, ly, lz) = diffs
            cross_a = vy * lz - vz * ly
            cross_b = vz * lx - vx * lz
            cross_c = vx * ly - vy * lx
            pen[slot[p]] = penalty_gain * (cross_a * cross_a + cross_b * cross_b + cross_c * cross_c)

    scale = 1.0 / (20.0 * math.sqrt(groups))

    def renew(part):
        for d in range(srcs - 1):
            if part == 0:
                label_copy(d).wait_recv()
            grad_copy(part, d).wait_recv()
        begin, count = parts[part]
        for s in range(begin, begin + count):
            p = [q for q in slot if slot[q] == s][0]
            own = acc[s, pl.ds(offset, band), :]
            grad_v = weight * own
            grad_c = (1.0 - weight) * own
            for d in range(srcs - 1):
                theirs = got[d, s]
                label = label_got[d, pl.ds(0, 1), :]
                grad_v = grad_v + label * theirs
                grad_c = grad_c + (1.0 - label) * theirs
            for m, grad in enumerate((grad_v, grad_c)):
                old = models[m, p, pl.ds(offset + PAD, band), :]
                value = old * jnp.exp(-step_size * jnp.tanh(scale * grad + pen[s]))
                fresh[m, s] = value
                updated[m, s, pl.ds(offset, band), :] = value
        for d in range(srcs - 1):
            fresh_copy(part, d).start()

    def take_models(part, chosen):
        for d in range(srcs - 1):
            fresh_wait(part, d)
        for p in chosen:
            form_coef(
                p,
                lambda p, r: updated[0, slot[p], pl.ds(r, rows), :],
                lambda p, r: updated[1, slot[p], pl.ds(r, rows), :],
            )

    for k in range(STEPS):
        interior(k, 0)
        if k == STEPS - 1:
            for d in range(srcs - 1):
                grad_copy(0, d).start()
        interior(k, 1)
        if k == 1:
            penalty()
        boundary(k, 0)
        if k == STEPS - 1:
            for d in range(srcs - 1):
                grad_copy(1, d).start()
        boundary(k, 1)

    renew(0)
    renew(1)
    take_models(0, inner)
    interior(STEPS, 0)
    interior(STEPS, 1)
    take_models(1, edge)
    boundary(STEPS, 0)
    boundary(STEPS, 1)
    for m in range(2):
        for p in range(planes):
            model_out_copy(m, p).start()
    for k in range(STEPS + 1, last):
        interior(k, 0)
        interior(k, 1)
        boundary(k, 0)
        boundary(k, 1)

    for side in range(2):
        @pl.when(sides[side][0])
        def _():
            for m in range(2):
                near_copy(m, side).wait_send()
            for k in range(last):
                for f in range(2):
                    halo_copy(k, f, side).wait_send()
    for d in range(srcs - 1):
        label_copy(d).wait_send()
        for part in range(2):
            grad_copy(part, d).wait_send()
            fresh_copy(part, d).wait_send()
    for p in range(planes):
        for f in range(2):
            out_copy(f, p).wait()
            model_out_copy(f, p).wait()


def shards(spaces, srcs, fields, velocity, conductivity, labels):
    planes, ny, nz = fields.shape[2:]
    band = ny // srcs
    last = 2 * STEPS
    groups = labels.shape[0] * srcs
    f32 = jnp.float32
    vmem = lambda *shape: pltpu.VMEM(shape, f32)
    dma = lambda *shape: pltpu.SemaphoreType.DMA(shape)
    anywhere = pl.BlockSpec(memory_space=pl.ANY)
    scratch = [
        vmem(last, 2, planes, ny + 2 * PAD, nz),
        vmem(2, planes, ny, nz),
        vmem(last, 2, 2, ny, nz),
        vmem(2, planes, ny + 2 * PAD, nz),
        vmem(2, 2, band, nz),
        vmem(2, planes, band + 2 * PAD, nz),
        vmem(planes, band, nz),
        vmem(planes, ny, nz),
        vmem(planes, ny, nz),
        vmem(srcs - 1, planes, band, nz),
        vmem(8, nz),
        vmem(srcs - 1, 8, nz),
        vmem(2, planes, band, nz),
        vmem(2, planes, ny, nz),
        vmem(2, planes, ny, nz),
        dma(4), dma(2), dma(4, planes),
        dma(last, 2, 2), dma(last, 2, 2), dma(2, 2), dma(2, 2),
        dma(srcs - 1), dma(srcs - 1), dma(2, srcs - 1), dma(2, srcs - 1), dma(2, srcs - 1), dma(2, srcs - 1),
    ]
    return tuple(pl.pallas_call(
        functools.partial(kernel, spaces, srcs, groups),
        out_shape=(
            jax.ShapeDtypeStruct((1, 2, planes, ny, nz), f32),
            jax.ShapeDtypeStruct((2, planes, ny, nz), f32),
        ),
        in_specs=[anywhere] * 3 + [pl.BlockSpec(memory_space=pltpu.SMEM)],
        out_specs=(anywhere, anywhere),
        scratch_shapes=scratch,
        cost_estimate=pl.CostEstimate(
            flops=40 * last * 2 * planes * ny * nz, bytes_accessed=40 * planes * ny * nz, transcendentals=0),
        compiler_params=pltpu.CompilerParams(
            collective_id=0, has_side_effects=True, vmem_limit_bytes=32 * 1024 * 1024),
    )(fields, velocity, conductivity, labels))


def solution(mesh):
    in_specs = (
        P(("parts", "src"), None, "space", None, None),
        P(("parts", "space"), None, None),
        P(("parts", "space"), None, None),
        P(("parts", "src")),
    )
    out_specs = (
        P(("parts", "src"), None, "space", None, None),
        P(None, ("parts", "space"), None, None),
    )
    body = functools.partial(shards, mesh.shape["space"], mesh.shape["src"])
    return jax.shard_map(body, mesh=mesh, in_specs=in_specs, out_specs=out_specs, check_vma=False)
```

time: 107 us -> 40.1 us (0.37)
  waiting for transfers between devices: 36.2 us -> 0 us
  starting transfers between devices: 34.9 us -> 0 us
  Pallas kernels: 0 us -> 33.9 us
  between operations: 15.1 us -> 1.3 us
  other arithmetic: 9.47 us -> 0 us
  blocking collectives: 6.77 us -> 0 us
    ppermute x14 -> x0, starting transfers between devices: 34.9 us -> none  [the longest x7 25.9 us: extended_2(): lax.ppermute(lax.slice_in_dim(block, block.shape[dim] - width, None, axis...]
    pallas_call x0 -> x1, Pallas kernels: none -> 33.9 us  [shards(): pl.pallas_call(functools.partial(kernel, spaces, srcs, groups), out_shape...]
    ppermute x14 -> x0, waiting for transfers between devices: 24.9 us -> none  [the longest x7 20.7 us: extended_2(): lax.ppermute(lax.slice_in_dim(block, 0, width, axis=dim), axis, backward)]
    reduce_scatter x1 -> x0, waiting for transfers between devices: 11.3 us -> none  [shards(): lax.psum_scatter(partial_sum, 'src', scatter_dimension=2, tiled=True)]
    all_gather x1 -> x0, blocking collectives: 6.77 us -> none  [shards(): updated = lax.all_gather(fresh, 'src', axis=2, tiled=True)]
    another operation x28 -> x0, other arithmetic: 5.28 us -> none  [the longest x21 2.26 us: advance_thin(): padded = extended_2(jnp.stack([upper, lower], 1), (('space', 2),), 1)]
    unnamed x7 -> x8, local copies, waits for them, and re-layouts: 1.8 us -> 4.71 us
    slice x4 -> x0, local copies, waits for them, and re-layouts: 2.1 us -> none  [the longest x1 1.07 us: shards(): state = (fields[:, 0], fields[:, 1], fields[:, 2], fields[:, 3])]
  transfers between devices with their start and end apart: 15 -> 0, of which waited for: 11 -> 0; matrix products, arithmetic and copies ran while one was open for 5% -> 0% of each run, Pallas kernels for 0% -> 0%
where the time goes in v1:
time: 40.1 us; the launch traced here: 39.9 us
  Pallas kernels  33.9 us (85%)
  local copies, waits for them, and re-layouts  4.71 us (12%)
  between operations  1.3 us (3%)
    pallas_call x1, Pallas kernels, shards(): pl.pallas_call(functools.partial(kernel, spaces, srcs, groups), out_shape...  33.9 us
    unnamed x8, local copies, waits for them, and re-layouts  4.71 us

profile of v1, /device:TPU:0, one launch (start us, length us, event | category | flops | bytes accessed | tf_op | source)
XLA Modules:
  0.0 39.9 jit_solution(7803274255179306390)
XLA Ops:
  1.3 0.0 copy-start
  1.3 1.2 %copy-done = f32[1,4,4,128,128]{4,3,2,1,0:T(8,128)S(1)} copy-done((f32[1,4,4,128,128]{4,3,2,1,0:T(8,128)S(1)}, f32[1,4,4,128,128]{4,3,2,1,0:T(8,128)}, u32[]{:S(2)}) %copy-start) | copy-done | bytes 1048600
  2.5 0.0 copy-start.1
  2.5 0.9 %copy-done.1 = f32[4,128,128]{2,1,0:T(8,128)S(1)} copy-done((f32[4,128,128]{2,1,0:T(8,128)S(1)}, f32[4,128,128]{2,1,0:T(8,128)}, u32[]{:S(2)}) %copy-start.1) | copy-done | bytes 262168
  3.5 0.0 copy-start.2
  3.5 0.9 %copy-done.2 = f32[4,128,128]{2,1,0:T(8,128)S(1)} copy-done((f32[4,128,128]{2,1,0:T(8,128)S(1)}, f32[4,128,128]{2,1,0:T(8,128)}, u32[]{:S(2)}) %copy-start.2) | copy-done | bytes 262168
  4.4 33.9 %shard_map.59 = (f32[1,2,4,128,128]{4,3,2,1,0:T(8,128)S(1)}, f32[2,4,128,128]{3,2,1,0:T(8,128)S(1)}) custom-call(f32[1,4,4,128,128]{4,3,2,1,0:T(8,128)S(1)} %copy-done, f32[4,128,128]{2,1,0:T(8,128)S(1)} %copy-done.1, f32[4,128,128]{2,1,0:T(8,128)S(1)} %copy-done.2, s32[1]{0:T(128)S(6)} %copy.8.labels), custom_call_target="tpu_custom_call" | custom-call | flops 31457280 | bytes 2621440 | tf_op jit(solution)/shard_map/pallas_call | solution.py:403
  38.3 0.8 %copy.9 = f32[1,2,4,128,128]{4,3,2,1,0:T(8,128)} copy(f32[1,2,4,128,128]{4,3,2,1,0:T(8,128)S(1)} %get-tuple-element.4) | data formatting | bytes 1048576
  39.1 0.8 %copy.10 = f32[2,4,128,128]{3,2,1,0:T(8,128)} copy(f32[2,4,128,128]{3,2,1,0:T(8,128)S(1)} %get-tuple-element.5) | data formatting | bytes 1048576
Async XLA Ops:
  1.3 1.2 %copy-start = (f32[1,4,4,128,128]{4,3,2,1,0:T(8,128)S(1)}, f32[1,4,4,128,128]{4,3,2,1,0:T(8,128)}, u32[]{:S(2)}) copy-start(f32[1,4,4,128,128]{4,3,2,1,0:T(8,128)} %fields.1) | copy-start | bytes 3145732
  2.5 0.9 %copy-start.1 = (f32[4,128,128]{2,1,0:T(8,128)S(1)}, f32[4,128,128]{2,1,0:T(8,128)}, u32[]{:S(2)}) copy-start(f32[4,128,128]{2,1,0:T(8,128)} %velocity.1) | copy-start | bytes 786436
  3.5 0.9 %copy-start.2 = (f32[4,128,128]{2,1,0:T(8,128)S(1)}, f32[4,128,128]{2,1,0:T(8,128)}, u32[]{:S(2)}) copy-start(f32[4,128,128]{2,1,0:T(8,128)} %conductivity.1) | copy-start | bytes 786436

commit v2 on v1

--- a/solution.py
+++ b/solution.py
@@ -26,7 +26,7 @@
     spaces, srcs, groups,
     fields, velocity, conductivity, labels,
     fields_out, models_out,
-    state, prev, halo, models, near, window, pen, coef, acc, got, label_own, label_got, fresh, updated, final,
+    state, prev, halo, models, near, window, pen, coef, acc, got, label_own, label_got, fresh, updated, ordered, final,
     load_sem, model_sem, out_sem,
     halo_send, halo_recv, near_send, near_recv,
     label_send, label_recv, grad_send, grad_recv, fresh_send, fresh_recv,
@@ -47,7 +47,7 @@
     slot = {p: p - 1 for p in inner}
     slot[0] = planes - 2
     slot[planes - 1] = planes - 1
-    parts = ((0, planes - 2), (planes - 2, 2))
+    parts = ((0, planes - 2), (planes - 2, 1), (planes - 1, 1))
 
     loads = []
     for f in range(2):
@@ -136,21 +136,21 @@
             send_sem=grad_send.at[part, d], recv_sem=grad_recv.at[part, d],
             device_id={"src": peers[d]}, device_id_type=MESH)
 
-    def fresh_copy(part, d):
+    def fresh_copy(kind, part, d):
         begin, count = parts[part]
         return pltpu.make_async_remote_copy(
-            src_ref=fresh.at[:, pl.ds(begin, count)],
-            dst_ref=updated.at[:, pl.ds(begin, count), pl.ds(offset, band), :],
-            send_sem=fresh_send.at[part, d], recv_sem=fresh_recv.at[part, d],
+            src_ref=fresh.at[kind, d, pl.ds(begin, count)],
+            dst_ref=updated.at[kind, pl.ds(begin, count), pl.ds(offset, band), :],
+            send_sem=fresh_send.at[kind, part, d], recv_sem=fresh_recv.at[kind, part, d],
             device_id={"src": peers[d]}, device_id_type=MESH)
 
-    def fresh_wait(part, d):
+    def fresh_wait(kind, part, d):
         begin, count = parts[part]
         source = pl.multiple_of(lax.rem(me + srcs - 1 - d, srcs) * band, 8)
-        ref = updated.at[:, pl.ds(begin, count), pl.ds(source, band), :]
+        ref = updated.at[kind, pl.ds(begin, count), pl.ds(source, band), :]
         pltpu.make_async_remote_copy(
             src_ref=ref, dst_ref=ref,
-            send_sem=fresh_send.at[part, d], recv_sem=fresh_recv.at[part, d],
+            send_sem=fresh_send.at[kind, part, d], recv_sem=fresh_recv.at[kind, part, d],
             device_id={"src": peers[d]}, device_id_type=MESH).wait_recv()
 
     halo_start(0, 0)
@@ -211,7 +211,7 @@
         return pltpu.make_async_copy(final.at[f, p], fields_out.at[0, f, p], out_sem.at[f, p])
 
     def model_out_copy(m, p):
-        return pltpu.make_async_copy(updated.at[m, slot[p]], models_out.at[m, p], out_sem.at[2 + m, p])
+        return pltpu.make_async_copy(ordered.at[m, p], models_out.at[m, p], out_sem.at[2 + m, p])
 
     def form_coef(p, velocity_at, conductivity_at):
         def body(r):
@@ -233,10 +233,12 @@
     for copy in loads:
         copy.wait()
 
-    def boundary(k, f):
+    def boundary(k, f, then=None):
         for side in range(2):
             halo_wait(k, f, side)
             advance(k, f, edge[side])
+            if then is not None:
+                then(side)
             if k + 1 < last:
                 @pl.when(sides[side][0])
                 def _():
@@ -288,9 +290,10 @@
     scale = 1.0 / (20.0 * math.sqrt(groups))
 
     def renew(part):
+        if part == 0:
+            for d in range(srcs - 1):
+                label_copy(d).wait_recv()
         for d in range(srcs - 1):
-            if part == 0:
-                label_copy(d).wait_recv()
             grad_copy(part, d).wait_recv()
         begin, count = parts[part]
         for s in range(begin, begin + count):
@@ -303,52 +306,84 @@
                 label = label_got[d, pl.ds(0, 1), :]
                 grad_v = grad_v + label * theirs
                 grad_c = grad_c + (1.0 - label) * theirs
+            new = []
             for m, grad in enumerate((grad_v, grad_c)):
                 old = models[m, p, pl.ds(offset + PAD, band), :]
-                value = old * jnp.exp(-step_size * jnp.tanh(scale * grad + pen[s]))
-                fresh[m, s] = value
-                updated[m, s, pl.ds(offset, band), :] = value
+                new.append(old * jnp.exp(-step_size * jnp.tanh(scale * grad + pen[s])))
+            for d in range(srcs):
+                label = weight if d == srcs - 1 else label_got[srcs - 2 - d, pl.ds(0, 1), :]
+                acoustic = jnp.broadcast_to(label, (band, nz)) > 0.5
+                needed = jnp.where(acoustic, new[0], new[1])
+                other = jnp.where(acoustic, new[1], new[0])
+                if d == srcs - 1:
+                    updated[0, s, pl.ds(offset, band), :] = needed
+                    updated[1, s, pl.ds(offset, band), :] = other
+                else:
+                    fresh[0, d, s] = needed
+                    fresh[1, d, s] = other
         for d in range(srcs - 1):
-            fresh_copy(part, d).start()
+            fresh_copy(0, part, d).start()
 
     def take_models(part, chosen):
         for d in range(srcs - 1):
-            fresh_wait(part, d)
+            fresh_wait(0, part, d)
         for p in chosen:
             form_coef(
                 p,
                 lambda p, r: updated[0, slot[p], pl.ds(r, rows), :],
-                lambda p, r: updated[1, slot[p], pl.ds(r, rows), :],
+                lambda p, r: updated[0, slot[p], pl.ds(r, rows), :],
             )
 
-    for k in range(STEPS):
+    def store_models():
+        for part in range(3):
+            for d in range(srcs - 1):
+                fresh_wait(1, part, d)
+        for p in range(planes):
+            def body(r):
+                needed = updated[0, slot[p], pl.ds(r, rows), :]
+                other = updated[1, slot[p], pl.ds(r, rows), :]
+                acoustic = jnp.full((rows, nz), weight) > 0.5
+                ordered[0, p, pl.ds(r, rows), :] = jnp.where(acoustic, needed, other)
+                ordered[1, p, pl.ds(r, rows), :] = jnp.where(acoustic, other, needed)
+            in_rows(body)
+            for m in range(2):
+                model_out_copy(m, p).start()
+
+    for k in range(STEPS - 1):
         interior(k, 0)
-        if k == STEPS - 1:
-            for d in range(srcs - 1):
-                grad_copy(0, d).start()
         interior(k, 1)
-        if k == 1:
+        if k == STEPS - 2:
             penalty()
         boundary(k, 0)
-        if k == STEPS - 1:
-            for d in range(srcs - 1):
-                grad_copy(1, d).start()
         boundary(k, 1)
 
+    def send_grad(part):
+        for d in range(srcs - 1):
+            grad_copy(part, d).start()
+
+    interior(STEPS - 1, 0)
+    send_grad(0)
+    interior(STEPS - 1, 1)
+    boundary(STEPS - 1, 0, lambda side: send_grad(1 + side))
     renew(0)
+    boundary(STEPS - 1, 1)
     renew(1)
+    renew(2)
     take_models(0, inner)
     interior(STEPS, 0)
     interior(STEPS, 1)
-    take_models(1, edge)
+    for side in range(2):
+        take_models(1 + side, edge[side:side + 1])
     boundary(STEPS, 0)
     boundary(STEPS, 1)
-    for m in range(2):
-        for p in range(planes):
-            model_out_copy(m, p).start()
+    for part in range(3):
+        for d in range(srcs - 1):
+            fresh_copy(1, part, d).start()
     for k in range(STEPS + 1, last):
         interior(k, 0)
         interior(k, 1)
+        if k == last - 1:
+            store_models()
         boundary(k, 0)
         boundary(k, 1)
 
@@ -362,9 +397,10 @@
                     halo_copy(k, f, side).wait_send()
     for d in range(srcs - 1):
         label_copy(d).wait_send()
-        for part in range(2):
+        for part in range(3):
             grad_copy(part, d).wait_send()
-            fresh_copy(part, d).wait_send()
+            for kind in range(2):
+                fresh_copy(kind, part, d).wait_send()
     for p in range(planes):
         for f in range(2):
             out_copy(f, p).wait()
@@ -393,12 +429,14 @@
         vmem(srcs - 1, planes, band, nz),
         vmem(8, nz),
         vmem(srcs - 1, 8, nz),
-        vmem(2, planes, band, nz),
+        vmem(2, srcs - 1, planes, band, nz),
+        vmem(2, planes, ny, nz),
         vmem(2, planes, ny, nz),
         vmem(2, planes, ny, nz),
         dma(4), dma(2), dma(4, planes),
         dma(last, 2, 2), dma(last, 2, 2), dma(2, 2), dma(2, 2),
-        dma(srcs - 1), dma(srcs - 1), dma(2, srcs - 1), dma(2, srcs - 1), dma(2, srcs - 1), dma(2, srcs - 1),
+        dma(srcs - 1), dma(srcs - 1), dma(3, srcs - 1), dma(3, srcs - 1),
+        dma(2, 3, srcs - 1), dma(2, 3, srcs - 1),
     ]
     return tuple(pl.pallas_call(
         functools.partial(kernel, spaces, srcs, groups),
@@ -406,13 +444,13 @@
             jax.ShapeDtypeStruct((1, 2, planes, ny, nz), f32),
             jax.ShapeDtypeStruct((2, planes, ny, nz), f32),
         ),
-        in_specs=[anywhere] * 3 + [pl.BlockSpec(memory_space=pltpu.SMEM)],
+        in_specs=[pl.BlockSpec(memory_space=pltpu.HBM)] * 3 + [pl.BlockSpec(memory_space=pltpu.SMEM)],
         out_specs=(anywhere, anywhere),
         scratch_shapes=scratch,
         cost_estimate=pl.CostEstimate(
             flops=40 * last * 2 * planes * ny * nz, bytes_accessed=40 * planes * ny * nz, transcendentals=0),
         compiler_params=pltpu.CompilerParams(
-            collective_id=0, has_side_effects=True, vmem_limit_bytes=32 * 1024 * 1024),
+            collective_id=0, has_side_effects=True, vmem_limit_bytes=56 * 1024 * 1024),
     )(fields, velocity, conductivity, labels))
 
 

time: 40.1 us -> 36 us (0.90)
  Pallas kernels: 33.9 us -> 31.8 us
  local copies, waits for them, and re-layouts: 4.71 us -> 2.73 us
    pallas_call x1, Pallas kernels: 33.9 us -> 31.8 us  [shards(): pl.pallas_call(functools.partial(kernel, spaces, srcs, groups), out_shape...]
    unnamed x8 -> x4, local copies, waits for them, and re-layouts: 4.71 us -> 2.73 us
where the time goes in v2:
time: 36 us; the launch traced here: 35.8 us
  Pallas kernels  31.8 us (88%)
  local copies, waits for them, and re-layouts  2.73 us (8%)
  between operations  1.29 us (4%)
    pallas_call x1, Pallas kernels, shards(): pl.pallas_call(functools.partial(kernel, spaces, srcs, groups), out_shape...  31.8 us
    unnamed x4, local copies, waits for them, and re-layouts  2.73 us

profile of v2, /device:TPU:0, one launch (start us, length us, event | category | flops | bytes accessed | tf_op | source)
XLA Modules:
  0.0 35.8 jit_solution(10890040997774562539)
XLA Ops:
  1.3 31.8 %shard_map.59 = (f32[1,2,4,128,128]{4,3,2,1,0:T(8,128)}, f32[2,4,128,128]{3,2,1,0:T(8,128)}) custom-call(f32[1,4,4,128,128]{4,3,2,1,0:T(8,128)} %fields.1, f32[4,128,128]{2,1,0:T(8,128)} %velocity.1, f32[4,128,128]{2,1,0:T(8,128)} %conductivity.1, s32[1]{0:T(128)S(6)} %copy.8.labels), custom_call_target="tpu_custom_call" | custom-call | flops 31457280 | bytes 2621440 | tf_op jit(solution)/shard_map/pallas_call | solution.py:441
  33.1 0.0 copy-start
  33.1 1.9 %copy.9 = f32[1,2,4,128,128]{4,3,2,1,0:T(8,128)} copy(f32[1,2,4,128,128]{4,3,2,1,0:T(8,128)} %get-tuple-element.4) | data formatting | bytes 1048576
  35.0 0.0 copy-done
  35.0 0.8 %copy.10 = f32[2,4,128,128]{3,2,1,0:T(8,128)} copy(f32[2,4,128,128]{3,2,1,0:T(8,128)S(1)} %copy-done) | data formatting | bytes 1048576
Async XLA Ops:
  33.1 1.9 %copy-start = (f32[2,4,128,128]{3,2,1,0:T(8,128)S(1)}, f32[2,4,128,128]{3,2,1,0:T(8,128)}, u32[]{:S(2)}) copy-start(f32[2,4,128,128]{3,2,1,0:T(8,128)} %get-tuple-element.5) | copy-start | bytes 1572868

commit v3 on v2

--- a/solution.py
+++ b/solution.py
@@ -10,6 +10,7 @@
 
 STEPS = 3
 PAD = 8
+PIECES = 2
 MESH = pl.DeviceIdType.MESH
 
 speed_gain = 0.25
@@ -26,14 +27,15 @@
     spaces, srcs, groups,
     fields, velocity, conductivity, labels,
     fields_out, models_out,
-    state, prev, halo, models, near, window, pen, coef, acc, got, label_own, label_got, fresh, updated, ordered, final,
-    load_sem, model_sem, out_sem,
+    state, prev, halo, models, near, window, pen, coef, acc, got, label_own, label_got, fresh, updated,
+    load_sem, model_sem,
     halo_send, halo_recv, near_send, near_recv,
     label_send, label_recv, grad_send, grad_recv, fresh_send, fresh_recv,
 ):
     planes, ny, nz = fields.shape[2:]
     band = ny // srcs
-    rows = 32 if ny % 32 == 0 else 8
+    piece = ny // PIECES
+    rows = 32 if piece % 32 == 0 else 8
     last = 2 * STEPS
     tile = lax.axis_index("space")
     me = lax.axis_index("src")
@@ -83,29 +85,31 @@
 
     pl.semaphore_wait(barrier, srcs - 1 + has_low.astype(jnp.int32) + has_high.astype(jnp.int32))
 
-    def halo_copy(k, f, side):
+    def halo_copy(k, f, side, i):
         plane = 0 if side == 0 else planes - 1
         if k == 0:
-            source = fields.at[0, 2 * f, plane]
+            source = fields.at[0, 2 * f, plane, pl.ds(i * piece, piece), :]
         else:
-            source = state.at[k, f, plane, pl.ds(PAD, ny), :]
+            source = state.at[k, f, plane, pl.ds(PAD + i * piece, piece), :]
         return pltpu.make_async_remote_copy(
-            src_ref=source, dst_ref=halo.at[k, f, 1 - side],
-            send_sem=halo_send.at[k, f, side], recv_sem=halo_recv.at[k, f, 1 - side],
+            src_ref=source, dst_ref=halo.at[k, f, 1 - side, pl.ds(i * piece, piece), :],
+            send_sem=halo_send.at[k, f, side, i], recv_sem=halo_recv.at[k, f, 1 - side, i],
             device_id={"space": sides[side][1]}, device_id_type=MESH)
 
     def halo_start(k, f):
-        for side in range(2):
-            @pl.when(sides[side][0])
-            def _():
-                halo_copy(k, f, side).start()
-
-    def halo_wait(k, f, side):
+        for i in range(PIECES):
+            for side in range(2):
+                @pl.when(sides[side][0])
+                def _():
+                    halo_copy(k, f, side, i).start()
+
+    def halo_wait(k, f, side, i):
         @pl.when(sides[side][0])
         def _():
+            ref = halo.at[k, f, side, pl.ds(i * piece, piece), :]
             pltpu.make_async_remote_copy(
-                src_ref=halo.at[k, f, side], dst_ref=halo.at[k, f, side],
-                send_sem=halo_send.at[k, f, side], recv_sem=halo_recv.at[k, f, side],
+                src_ref=ref, dst_ref=ref,
+                send_sem=halo_send.at[k, f, side, i], recv_sem=halo_recv.at[k, f, side, i],
                 device_id={"space": sides[side][1]}, device_id_type=MESH).wait_recv()
 
     def near_copy(m, side):
@@ -170,15 +174,15 @@
                 for f in range(2):
                     halo[k, f, side] = jnp.zeros((ny, nz), jnp.float32)
 
-    def in_rows(body):
+    def in_rows(body, begin=0, count=ny):
         def step(i, carry):
-            body(pl.multiple_of(i * rows, 8))
+            body(pl.multiple_of(begin + i * rows, 8))
             return carry
-        lax.fori_loop(0, ny // rows, step, 0, unroll=True)
+        lax.fori_loop(0, count // rows, step, 0, unroll=True)
 
     keep_gain = 1.0 + weight
 
-    def advance(k, f, p):
+    def advance(k, f, p, begin=0, count=ny):
         def body(r):
             def at(plane, shift):
                 return state[k, f, plane, pl.ds(r + PAD + shift, rows), :]
@@ -202,16 +206,10 @@
                 before = state[k - 1, f, p, pl.ds(r + PAD, rows), :]
             value = keep_gain * middle - weight * before + coef[slot[p], pl.ds(r, rows), :] * lap
             if k == last - 1:
-                final[f, p, pl.ds(r, rows), :] = value
+                fields_out[0, f, p, pl.ds(r, rows), :] = value
             else:
                 state[k + 1, f, p, pl.ds(r + PAD, rows), :] = value
-        in_rows(body)
-
-    def out_copy(f, p):
-        return pltpu.make_async_copy(final.at[f, p], fields_out.at[0, f, p], out_sem.at[f, p])
-
-    def model_out_copy(m, p):
-        return pltpu.make_async_copy(ordered.at[m, p], models_out.at[m, p], out_sem.at[2 + m, p])
+        in_rows(body, begin, count)
 
     def form_coef(p, velocity_at, conductivity_at):
         def body(r):
@@ -234,23 +232,20 @@
         copy.wait()
 
     def boundary(k, f, then=None):
-        for side in range(2):
-            halo_wait(k, f, side)
-            advance(k, f, edge[side])
-            if then is not None:
-                then(side)
-            if k + 1 < last:
-                @pl.when(sides[side][0])
-                def _():
-                    halo_copy(k + 1, f, side).start()
-            else:
-                out_copy(f, edge[side]).start()
+        for i in range(PIECES):
+            for side in range(2):
+                halo_wait(k, f, side, i)
+                advance(k, f, edge[side], i * piece, piece)
+                if k + 1 < last:
+                    @pl.when(sides[side][0])
+                    def _():
+                        halo_copy(k + 1, f, side, i).start()
+                if then is not None and i == PIECES - 1:
+                    then(side)
 
     def interior(k, f):
         for p in inner:
             advance(k, f, p)
-            if k == last - 1:
-                out_copy(f, p).start()
 
     def penalty():
         def prepare(p, carry):
@@ -343,11 +338,9 @@
                 needed = updated[0, slot[p], pl.ds(r, rows), :]
                 other = updated[1, slot[p], pl.ds(r, rows), :]
                 acoustic = jnp.full((rows, nz), weight) > 0.5
-                ordered[0, p, pl.ds(r, rows), :] = jnp.where(acoustic, needed, other)
-                ordered[1, p, pl.ds(r, rows), :] = jnp.where(acoustic, other, needed)
+                models_out[0, p, pl.ds(r, rows), :] = jnp.where(acoustic, needed, other)
+                models_out[1, p, pl.ds(r, rows), :] = jnp.where(acoustic, other, needed)
             in_rows(body)
-            for m in range(2):
-                model_out_copy(m, p).start()
 
     for k in range(STEPS - 1):
         interior(k, 0)
@@ -394,17 +387,14 @@
                 near_copy(m, side).wait_send()
             for k in range(last):
                 for f in range(2):
-                    halo_copy(k, f, side).wait_send()
+                    for i in range(PIECES):
+                        halo_copy(k, f, side, i).wait_send()
     for d in range(srcs - 1):
         label_copy(d).wait_send()
         for part in range(3):
             grad_copy(part, d).wait_send()
             for kind in range(2):
                 fresh_copy(kind, part, d).wait_send()
-    for p in range(planes):
-        for f in range(2):
-            out_copy(f, p).wait()
-            model_out_copy(f, p).wait()
 
 
 def shards(spaces, srcs, fields, velocity, conductivity, labels):
@@ -431,21 +421,19 @@
         vmem(srcs - 1, 8, nz),
         vmem(2, srcs - 1, planes, band, nz),
         vmem(2, planes, ny, nz),
-        vmem(2, planes, ny, nz),
-        vmem(2, planes, ny, nz),
-        dma(4), dma(2), dma(4, planes),
-        dma(last, 2, 2), dma(last, 2, 2), dma(2, 2), dma(2, 2),
+        dma(4), dma(2),
+        dma(last, 2, 2, PIECES), dma(last, 2, 2, PIECES), dma(2, 2), dma(2, 2),
         dma(srcs - 1), dma(srcs - 1), dma(3, srcs - 1), dma(3, srcs - 1),
         dma(2, 3, srcs - 1), dma(2, 3, srcs - 1),
     ]
     return tuple(pl.pallas_call(
         functools.partial(kernel, spaces, srcs, groups),
         out_shape=(
-            jax.ShapeDtypeStruct((1, 2, planes, ny, nz), f32),
-            jax.ShapeDtypeStruct((2, planes, ny, nz), f32),
+            pltpu.VMEM((1, 2, planes, ny, nz), f32),
+            pltpu.VMEM((2, planes, ny, nz), f32),
         ),
         in_specs=[pl.BlockSpec(memory_space=pltpu.HBM)] * 3 + [pl.BlockSpec(memory_space=pltpu.SMEM)],
-        out_specs=(anywhere, anywhere),
+        out_specs=(pl.BlockSpec(memory_space=pltpu.VMEM),)*2,
         scratch_shapes=scratch,
         cost_estimate=pl.CostEstimate(
             flops=40 * last * 2 * planes * ny * nz, bytes_accessed=40 * planes * ny * nz, transcendentals=0),

time: 36 us -> 34.4 us (0.956)
  local copies, waits for them, and re-layouts: 2.73 us -> 1.59 us
  Pallas kernels: 31.8 us -> 31.4 us
    unnamed x4 -> x2, local copies, waits for them, and re-layouts: 2.73 us -> 1.59 us
    pallas_call x1, Pallas kernels: 31.8 us -> 31.4 us  [shards(): pl.pallas_call(functools.partial(kernel, spaces, srcs, groups), out_shape...]
where the time goes in v3:
time: 34.4 us; the launch traced here: 34.2 us
  Pallas kernels  31.4 us (91%)
  local copies, waits for them, and re-layouts  1.59 us (5%)
  between operations  1.29 us (4%)
    pallas_call x1, Pallas kernels, shards(): pl.pallas_call(functools.partial(kernel, spaces, srcs, groups), out_shape...  31.4 us
    unnamed x2, local copies, waits for them, and re-layouts  1.59 us

profile of v3, /device:TPU:0, one launch (start us, length us, event | category | flops | bytes accessed | tf_op | source)
XLA Modules:
  0.0 34.2 jit_solution(3328264224381564107)
XLA Ops:
  1.3 31.4 %shard_map.59 = (f32[1,2,4,128,128]{4,3,2,1,0:T(8,128)S(1)}, f32[2,4,128,128]{3,2,1,0:T(8,128)S(1)}) custom-call(f32[1,4,4,128,128]{4,3,2,1,0:T(8,128)} %fields.1, f32[4,128,128]{2,1,0:T(8,128)} %velocity.1, f32[4,128,128]{2,1,0:T(8,128)} %conductivity.1, s32[1]{0:T(128)S(6)} %copy.10.labels), custom_call_target="tpu_custom_call" | custom-call | flops 31457280 | bytes 2621440 | tf_op jit(solution)/shard_map/pallas_call | solution.py:429
  32.7 0.8 %copy.8 = f32[1,2,4,128,128]{4,3,2,1,0:T(8,128)} copy(f32[1,2,4,128,128]{4,3,2,1,0:T(8,128)S(1)} %get-tuple-element.2) | data formatting | bytes 1048576
  33.4 0.8 %copy.9 = f32[2,4,128,128]{3,2,1,0:T(8,128)} copy(f32[2,4,128,128]{3,2,1,0:T(8,128)S(1)} %get-tuple-element.3) | data formatting | bytes 1048576

commit v4 on v3

--- a/solution.py
+++ b/solution.py
@@ -342,20 +342,20 @@
                 models_out[1, p, pl.ds(r, rows), :] = jnp.where(acoustic, other, needed)
             in_rows(body)
 
+    def send_grad(part):
+        for d in range(srcs - 1):
+            grad_copy(part, d).start()
+
+    interior(0, 0)
     for k in range(STEPS - 1):
-        interior(k, 0)
         interior(k, 1)
         if k == STEPS - 2:
             penalty()
         boundary(k, 0)
+        interior(k + 1, 0)
+        if k == STEPS - 2:
+            send_grad(0)
         boundary(k, 1)
-
-    def send_grad(part):
-        for d in range(srcs - 1):
-            grad_copy(part, d).start()
-
-    interior(STEPS - 1, 0)
-    send_grad(0)
     interior(STEPS - 1, 1)
     boundary(STEPS - 1, 0, lambda side: send_grad(1 + side))
     renew(0)

time: 34.4 us -> 33.8 us (0.983)
  Pallas kernels: 31.4 us -> 30.8 us
    pallas_call x1, Pallas kernels: 31.4 us -> 30.8 us  [shards(): pl.pallas_call(functools.partial(kernel, spaces, srcs, groups), out_shape...]
where the time goes in v4:
time: 33.8 us; the launch traced here: 33.6 us
  Pallas kernels  30.8 us (91%)
  local copies, waits for them, and re-layouts  1.59 us (5%)
  between operations  1.29 us (4%)
    pallas_call x1, Pallas kernels, shards(): pl.pallas_call(functools.partial(kernel, spaces, srcs, groups), out_shape...  30.8 us
    unnamed x2, local copies, waits for them, and re-layouts  1.59 us

profile of v4, /device:TPU:0, one launch (start us, length us, event | category | flops | bytes accessed | tf_op | source)
XLA Modules:
  0.0 33.6 jit_solution(2052957092603981505)
XLA Ops:
  1.3 30.8 %shard_map.59 = (f32[1,2,4,128,128]{4,3,2,1,0:T(8,128)S(1)}, f32[2,4,128,128]{3,2,1,0:T(8,128)S(1)}) custom-call(f32[1,4,4,128,128]{4,3,2,1,0:T(8,128)} %fields.1, f32[4,128,128]{2,1,0:T(8,128)} %velocity.1, f32[4,128,128]{2,1,0:T(8,128)} %conductivity.1, s32[1]{0:T(128)S(6)} %copy.10.labels), custom_call_target="tpu_custom_call" | custom-call | flops 31457280 | bytes 2621440 | tf_op jit(solution)/shard_map/pallas_call | solution.py:429
  32.1 0.8 %copy.8 = f32[1,2,4,128,128]{4,3,2,1,0:T(8,128)} copy(f32[1,2,4,128,128]{4,3,2,1,0:T(8,128)S(1)} %get-tuple-element.2) | data formatting | bytes 1048576
  32.9 0.8 %copy.9 = f32[2,4,128,128]{3,2,1,0:T(8,128)} copy(f32[2,4,128,128]{3,2,1,0:T(8,128)S(1)} %get-tuple-element.3) | data formatting | bytes 1048576
